TPU v7x, 32 devices: a whole 2x2x4 slice. The times are simulated.
32 devices in a mesh: samp: 8 (over z, y), feat: 4 (over x, core).
Axes of the slice: x: 2, y: 2, z: 4, core: 2. Of those that a mesh axis runs over, the one named last changes fastest.
Arguments:
- states: bfloat16 [8192, 16384], P('samp', 'feat'), may hold values from -0.176776695 to 0.176776695
- targets: float32 [8192, 128], P('samp'), may hold values from -40 to 40
- penalty: float32 [128], replicated, may hold values from 0.1 to 1
Outputs:
- readout: float32 [16384, 128], P('feat')
- residual: float32 [8192, 128], P('samp')
All inputs are finite; a program needn't handle non-finite values.
Results may differ from a plain program's by a relative error of at most 0.0058.
Values may be sent and summed in bfloat16 or wider, within the bound.
A program may use at most 64 MiB of HBM per device.

v0:
```python
import jax
import jax.numpy as jnp
from jax import lax
from jax.sharding import PartitionSpec as P

ITERS = 3


def shards(states, targets, penalty):
    feat_rows = states.shape[1]

    def weight_sum(value):
        return lax.psum(value, "feat")

    def gradient_of(residual, readout):
        residual_b = residual.astype(jnp.bfloat16)
        partial_value = lax.dot_general(
            states, residual_b, (((0,), (0,)), ((), ())), preferred_element_type=jnp.float32
        )
        summed = lax.psum(partial_value, "samp")
        return summed - penalty * readout

    readout = jnp.zeros((feat_rows, targets.shape[1]), jnp.float32)
    residual = targets
    gradient = gradient_of(residual, readout)
    direction = gradient
    norm_now = weight_sum(jnp.sum(gradient * gradient, axis=0))
    for step in range(ITERS):
        direction_b = direction.astype(jnp.bfloat16)
        image_partial_value = jnp.dot(states, direction_b, preferred_element_type=jnp.float32)
        image = lax.psum(image_partial_value, "feat")
        image_sq = jnp.sum(image * image, axis=0)
        direction_sq = jnp.sum(direction * direction, axis=0)
        curvature = lax.psum(image_sq, "samp") + penalty * weight_sum(direction_sq)
        step_size = norm_now / curvature
        readout = readout + step_size * direction
        residual = residual - step_size * image
        if step + 1 < ITERS:
            gradient = gradient_of(residual, readout)
            norm_next = weight_sum(jnp.sum(gradient * gradient, axis=0))
            direction = gradient + norm_next / norm_now * direction
            norm_now = norm_next
    return (readout, residual)


def solution(mesh):
    in_specs = (P("samp", "feat"), P("samp", None), P())
    out_specs = (P("feat", None), P("samp", None))
    return jax.shard_map(shards, mesh=mesh, in_specs=in_specs, out_specs=out_specs, check_vma=False)
```

profile of v0, /device:TPU:0, one launch (start us, length us, event | category | flops | bytes accessed | tf_op | source)
XLA Modules:
  0.0 558.5 jit_solution(16675980969986547672)
XLA Ops:
  7.2 7.1 %fusion.5 = f32[4096,128]{1,0:T(8,128)} fusion(bf16[1024,4096]{1,0:T(8,128)(2,1)} %param.3, f32[1024,128]{1,0:T(8,128)} %param.4), kind=kOutput, calls=%fused_computation.28 | convolution fusion | flops 1073872896 | bytes 11010048 | tf_op jit(solution)/shard_map/dot_general | solution.py:17
  15.0 104.0 %all-reduce.7.cloned.1.call-done = f32[4096,128]{1,0:T(8,128)} async-done(((f32[4096,128]{1,0:T(8,128)}), f32[4096,128]{1,0:T(8,128)}) %all-reduce.7.cloned.1.call-update) | async-done | bytes 2097168 | tf_op jit(solution)/shard_map/psum | solution.py:20
  119.0 7.8 %convolution_bitcast_fusion.4 = f32[1024,128]{0,1:T(8,128)} fusion(bf16[1024,4096]{1,0:T(8,128)(2,1)} %param.3, f32[4096,128]{1,0:T(8,128)} %all-reduce.7.cloned.1.call-done, f32[128]{0:T(128)S(1)} %broadcast_multiply_fusion), kind=kOutput, calls=%fused_computation.16 | convolution fusion | flops 1074790400 | bytes 11010560 | tf_op jit(solution)/shard_map/dot_general | solution.py:30
  127.7 6.3 %psum.102 = f32[128]{0:T(128)S(1)} all-reduce(f32[128]{0:T(128)S(1)} %multiply_reduce_fusion.4), channel_id=1, replica_groups=mesh['samp'=8,'feat'=4] {'feat'}, use_global_device_ids=true, to_apply=%region_2.0 | all-reduce | flops 128 | bytes 1024 | tf_op jit(solution)/shard_map/psum | solution.py:13
  134.0 25.9 %all-reduce.9.cloned.1.call-done = f32[1024,128]{0,1:T(8,128)} async-done(((f32[1024,128]{0,1:T(8,128)}), f32[1024,128]{0,1:T(8,128)}) %all-reduce.9.cloned.1.call-update) | async-done | bytes 524304 | tf_op jit(solution)/shard_map/psum | solution.py:31
  161.1 21.4 %psum.104 = f32[128]{0:T(128)S(1)} all-reduce(f32[128]{0:T(128)S(1)} %multiply_reduce_fusion.7), channel_id=1, replica_groups=mesh['samp'=8,'feat'=4] {'samp'}, use_global_device_ids=true, to_apply=%region_5.0 | all-reduce | flops 128 | bytes 1024 | tf_op jit(solution)/shard_map/psum | solution.py:34
  182.5 8.3 %convolution_bitcast_fusion.1 = f32[4096,128]{1,0:T(8,128)} fusion(bf16[1024,4096]{1,0:T(8,128)(2,1)} %param.3, f32[1024,128]{0,1:T(8,128)S(1)} %copy.5, f32[1024,128]{0,1:T(8,128)} %all-reduce.9.cloned.1.call-done, f32[128]{0:T(128)S(1)} %add_divide_fusion.2), kind=kOutput, calls=%fused_computation.1 | convolution fusion | flops 1074135040 | bytes 11534848 | tf_op jit(solution)/shard_map/dot_general | solution.py:17
  190.8 98.2 %all-reduce.11.cloned.1.call-done = f32[4096,128]{1,0:T(8,128)} async-done(((f32[4096,128]{1,0:T(8,128)}), f32[4096,128]{1,0:T(8,128)}) %all-reduce.11.cloned.1.call-update) | async-done | bytes 2097168 | tf_op jit(solution)/shard_map/psum | solution.py:20
  291.1 6.5 %psum.106 = f32[128]{0:T(128)S(1)} all-reduce(f32[128]{0:T(128)S(1)} %multiply_reduce_fusion.3), channel_id=1, replica_groups=mesh['samp'=8,'feat'=4] {'feat'}, use_global_device_ids=true, to_apply=%region_8.0 | all-reduce | flops 128 | bytes 1024 | tf_op jit(solution)/shard_map/psum | solution.py:13
  297.6 7.7 %convolution_bitcast_fusion.3 = f32[1024,128]{0,1:T(8,128)} fusion(bf16[1024,4096]{1,0:T(8,128)(2,1)} %param.3, f32[4096,128]{1,0:T(8,128)} %all-reduce.11.cloned.1.call-done, f32[4096,128]{1,0:T(8,128)S(1)} %copy-done, f32[128]{0:T(128)S(1)} %div.16, f32[128]{0:T(128)S(1)} %copy-done.6, f32[128]{0:T(128)S(1)} %add_divide_fusion.2, ...), kind=kOutput, calls=%fused_computation.15 | convolution fusion | flops 1077411840 | bytes 13109248 | tf_op jit(solution)/shard_map/dot_general | solution.py:30
  305.4 2.2 multiply_reduce_fusion.2
  307.6 5.9 %psum.109 = f32[128]{0:T(128)S(1)} all-reduce(f32[128]{0:T(128)S(1)} %multiply_reduce_fusion.2), channel_id=1, replica_groups=mesh['samp'=8,'feat'=4] {'feat'}, use_global_device_ids=true, to_apply=%region_13.0 | all-reduce | flops 128 | bytes 1024 | tf_op jit(solution)/shard_map/psum | solution.py:13
  313.6 24.5 %all-reduce.13.cloned.1.call-done = f32[1024,128]{0,1:T(8,128)} async-done(((f32[1024,128]{0,1:T(8,128)}), f32[1024,128]{0,1:T(8,128)}) %all-reduce.13.cloned.1.call-update) | async-done | bytes 524304 | tf_op jit(solution)/shard_map/psum | solution.py:31
  339.3 21.4 %psum.108 = f32[128]{0:T(128)S(1)} all-reduce(f32[128]{0:T(128)S(1)} %multiply_reduce_fusion.6), channel_id=1, replica_groups=mesh['samp'=8,'feat'=4] {'samp'}, use_global_device_ids=true, to_apply=%region_11.0 | all-reduce | flops 128 | bytes 1024 | tf_op jit(solution)/shard_map/psum | solution.py:34
  362.7 8.1 %convolution_bitcast_fusion = f32[4096,128]{1,0:T(8,128)} fusion(bf16[1024,4096]{1,0:T(8,128)(2,1)} %param.3, f32[1024,128]{0,1:T(8,128)S(1)} %multiply_subtract_fusion.3), kind=kOutput, calls=%fused_computation | convolution fusion | flops 1073872896 | bytes 11010048 | tf_op jit(solution)/shard_map/dot_general | solution.py:17
  370.8 98.2 %all-reduce.15.cloned.1.call-done = f32[4096,128]{1,0:T(8,128)} async-done(((f32[4096,128]{1,0:T(8,128)}), f32[4096,128]{1,0:T(8,128)}) %all-reduce.15.cloned.1.call-update) | async-done | bytes 2097168 | tf_op jit(solution)/shard_map/psum | solution.py:20
  469.0 3.1 multiply_reduce_fusion.1
  472.0 6.3 %psum.111 = f32[128]{0:T(128)S(1)} all-reduce(f32[128]{0:T(128)S(1)} %multiply_reduce_fusion.1), channel_id=1, replica_groups=mesh['samp'=8,'feat'=4] {'feat'}, use_global_device_ids=true, to_apply=%region_16.0 | all-reduce | flops 128 | bytes 1024 | tf_op jit(solution)/shard_map/psum | solution.py:13
  478.4 3.2 multiply_reduce_fusion
  482.9 7.1 %convolution_bitcast_fusion.2 = f32[1024,128]{0,1:T(8,128)} fusion(bf16[1024,4096]{1,0:T(8,128)(2,1)} %param.3, f32[4096,128]{1,0:T(8,128)S(1)} %get-tuple-element.5), kind=kOutput, calls=%fused_computation.14 | convolution fusion | flops 1074266112 | bytes 11010048 | tf_op jit(solution)/shard_map/dot_general | solution.py:30
  490.0 5.9 %psum.114 = f32[128]{0:T(128)S(1)} all-reduce(f32[128]{0:T(128)S(1)} %get-tuple-element.4), channel_id=1, replica_groups=mesh['samp'=8,'feat'=4] {'feat'}, use_global_device_ids=true, to_apply=%region_21.0 | all-reduce | flops 128 | bytes 1024 | tf_op jit(solution)/shard_map/psum | solution.py:13
  496.0 26.7 %all-reduce.17.cloned.1.call-done = f32[1024,128]{0,1:T(8,128)} async-done(((f32[1024,128]{0,1:T(8,128)}), f32[1024,128]{0,1:T(8,128)}) %all-reduce.17.cloned.1.call-update) | async-done | bytes 524304 | tf_op jit(solution)/shard_map/psum | solution.py:31
  523.9 21.4 %psum.113 = f32[128]{0:T(128)S(1)} all-reduce(f32[128]{0:T(128)S(1)} %multiply_reduce_fusion.5), channel_id=1, replica_groups=mesh['samp'=8,'feat'=4] {'samp'}, use_global_device_ids=true, to_apply=%region_19.0 | all-reduce | flops 128 | bytes 1024 | tf_op jit(solution)/shard_map/psum | solution.py:34
  547.4 4.2 multiply_add_fusion
  (41 shorter events, 12.8 us)
Async XLA Ops:
  7.2 111.8 %all-reduce.7.cloned.1.call-start = ((), (), s32[]{:S(2)}) async-start(), calls=%async_computation | async-start | bytes 4194304 | tf_op jit(solution)/shard_map/psum | solution.py:20
  14.3 0.7 copy-start.6
  14.4 145.6 %all-reduce.9.cloned.1.call-start = ((), (), s32[]{:S(2)}) async-start(), calls=%async_computation.1 | async-start | bytes 1048576 | tf_op jit(solution)/shard_map/psum | solution.py:31
  15.0 111.9 %copy-start.5 = (f32[1024,128]{1,0:T(8,128)S(1)}, f32[1024,128]{1,0:T(8,128)}, u32[]{:S(2)}) copy-start(f32[1024,128]{1,0:T(8,128)} %param.4) | copy-start | bytes 1572868
  119.0 8.1 %copy-start = (f32[4096,128]{1,0:T(8,128)S(1)}, f32[4096,128]{1,0:T(8,128)}, u32[]{:S(2)}) copy-start(f32[4096,128]{1,0:T(8,128)} %all-reduce.7.cloned.1.call-done) | copy-start | bytes 6291460
  126.9 162.1 %all-reduce.11.cloned.1.call-start = ((), (), s32[]{:S(2)}) async-start(), calls=%async_computation.2 | async-start | bytes 4194304 | tf_op jit(solution)/shard_map/psum | solution.py:20
  190.8 147.3 %all-reduce.13.cloned.1.call-start = ((), (), s32[]{:S(2)}) async-start(), calls=%async_computation.3 | async-start | bytes 1048576 | tf_op jit(solution)/shard_map/psum | solution.py:31
  305.4 55.3 %copy-start.2 = (f32[1024,128]{0,1:T(8,128)S(1)}, f32[1024,128]{0,1:T(8,128)}, u32[]{:S(2)}) copy-start(f32[1024,128]{0,1:T(8,128)} %all-reduce.9.cloned.1.call-done) | copy-start | bytes 1572868
  305.4 163.6 %all-reduce.15.cloned.1.call-start = ((), (), s32[]{:S(2)}) async-start(), calls=%async_computation.4 | async-start | bytes 4194304 | tf_op jit(solution)/shard_map/psum | solution.py:20
  361.9 0.8 copy-start.3
  370.8 151.9 %all-reduce.17.cloned.1.call-start = ((), (), s32[]{:S(2)}) async-start(), calls=%async_computation.5 | async-start | bytes 1048576 | tf_op jit(solution)/shard_map/psum | solution.py:31
  481.6 1.3 copy-start.1
  482.9 62.4 %copy-start.4 = (f32[1024,128]{0,1:T(8,128)S(1)}, f32[1024,128]{0,1:T(8,128)}, u32[]{:S(2)}) copy-start(f32[1024,128]{0,1:T(8,128)} %copy-done.3) | copy-start | bytes 1572868
Sparse Core Ops, SparseCore 0:
  14.5 104.4 all-reduce.6
  127.0 32.8 all-reduce.8
  190.9 98.0 all-reduce.10
  305.5 32.5 all-reduce.12
  370.9 98.0 all-reduce.14
  490.1 32.5 all-reduce.16
where the time goes:
time: 559 us; the launch traced here: 558 us
  waiting for transfers between devices  378 us (68%)
  blocking collectives  95.1 us (17%)
  matrix products  46.2 us (8%)
  other arithmetic  21.3 us (4%)
  between operations  14.2 us (3%)
    psum x3, waiting for transfers between devices, gradient_of(): summed = lax.psum(partial_value, 'samp')  300 us
    psum x3, waiting for transfers between devices, shards(): image = lax.psum(image_partial_value, 'feat')  77.2 us
    psum x3, blocking collectives, shards(): curvature = lax.psum(image_sq, 'samp') + penalty * weight_sum(direction_sq)  64.1 us
    psum x5, blocking collectives, weight_sum(): return lax.psum(value, 'feat')  31 us
    dot_general x3, matrix products, gradient_of(): lax.dot_general(states, residual_b, (((0,), (0,)), ((), ())), preferred_e...  23.5 us
    dot_general x3, matrix products, shards(): jnp.dot(states, direction_b, preferred_element_type=jnp.float32)  22.7 us
  transfers between devices with their start and end apart: 6, of which 6 were waited for; matrix products, arithmetic and copies ran while one was open for 1% of the time, Pallas kernels for 0%

commit v1 on v0

v1 whole, which is shorter than its diff:
```python
import functools
import jax
import jax.numpy as jnp
from jax import lax
from jax.experimental import pallas as pl
from jax.experimental.pallas import tpu as pltpu
from jax.sharding import PartitionSpec as P

ITERS = 3
F32 = jnp.float32
BF16 = jnp.bfloat16


def flip(index, mask):
    out = index
    bit = 1
    while bit <= mask:
        if mask & bit:
            out = out + bit - 2 * bit * ((index // bit) % 2)
        bit *= 2
    return out


def to_rows(columns):
    channels = columns[0].shape[0]
    lane = lax.broadcasted_iota(jnp.int32, (channels, 128), 1)
    block = jnp.zeros((channels, 128), F32)
    for i, column in enumerate(columns):
        block = jnp.where(lane == i, column, block)
    return jnp.transpose(block)[:8]


def to_columns(rows, count):
    channels = rows.shape[1]
    block = jnp.concatenate([rows, jnp.zeros((128 - 8, channels), F32)], axis=0)
    block = jnp.transpose(block)
    return [block[:, i : i + 1] for i in range(count)]


def kernel(
    n_samp, a_hbm, t_ref, pen_ref, x_out, r_out,
    a, vb, r, acc, rs_send, rs_recv, ag, d, x, qa, q, sm, cu,
    c1_send, c1_recv, c1s_send, c1s_recv, x2_send, x2_recv, x2s_send, x2s_recv, c3_recv,
    a_sem, rs_ss, rs_rs, ag_ss, ag_rs, sm_ss, sm_rs, cu_ss, cu_rs, f_ss, f_rs,
):
    chunk = a.shape[2]
    half = a.shape[1] // 2
    me = lax.axis_index("samp")
    feat = lax.axis_index("feat")
    core = feat % 2
    peers = sorted(range(1, n_samp), key=lambda o: (-(o // 4), o))
    near = list(range(1, n_samp))
    other_core = {"feat": flip(feat, 1)}
    other_x = {"feat": flip(feat, 2)}

    def load(o, h):
        rows = pl.ds(pl.multiple_of(flip(core, h) * half, half), half)
        columns = pl.ds(pl.multiple_of(flip(me, o) * chunk, chunk), chunk)
        return pltpu.make_async_copy(
            a_hbm.at[rows, columns], a.at[o, pl.ds(h * half, half)], a_sem.at[o, h]
        )

    for o in peers + [0]:
        for h in range(2):
            load(o, h).start()

    barrier = pltpu.get_barrier_semaphore()
    for o in near:
        pl.semaphore_signal(barrier, inc=1, device_id={"samp": flip(me, o)})
    for partner in (other_core, other_x):
        pl.semaphore_signal(barrier, inc=1, device_id=partner)

    pen = pen_ref[...]
    for h in range(2):
        r[h] = t_ref[:, pl.ds(pl.multiple_of(flip(core, h) * half, half), half)]
    d[...] = jnp.zeros_like(d)
    x[...] = jnp.zeros_like(x)
    q[...] = jnp.zeros_like(q)
    pl.semaphore_wait(barrier, n_samp - 1 + 2)

    def send(src, dst, ss, rs, target):
        copy = pltpu.make_async_remote_copy(
            src_ref=src, dst_ref=dst, send_sem=ss, recv_sem=rs, device_id=target,
        )
        copy.start()
        return copy

    def row_sum(value):
        return jnp.sum(value, axis=1, keepdims=True)

    def advance(o, last, alpha, beta):
        new = ag[last, o].astype(F32) + beta * d[o]
        d[o] = new
        x[o] = x[o] + alpha * new

    def step(k, carry):
        norm, dsq, alpha, beta = carry
        for h in range(2):
            vb[:, h * half : (h + 1) * half] = r[h].astype(BF16)

        def project(o):
            @pl.when(k == 0)
            def _():
                for h in range(2):
                    load(o, h).wait()

            return jnp.dot(vb[...], a[o], preferred_element_type=F32)

        sent = {}
        for o in peers:
            rs_send[o] = project(o).astype(BF16)
            sent[o] = send(
                rs_send.at[o], rs_recv.at[k, o], rs_ss.at[o], rs_rs.at[k, o], {"samp": flip(me, o)}
            )
        acc[...] = project(0)

        @pl.when(k > 0)
        def _():
            for o in range(n_samp):
                advance(o, k - 1, alpha, beta)

        for o in near:
            sent[o].wait_recv()
            acc[...] += rs_recv[k, o].astype(F32)
        g = acc[...] - pen * x[0]
        gb = g.astype(BF16)
        ag[k, 0] = gb
        gathered, small = {}, {}
        for o in peers:
            gathered[o] = send(
                ag.at[k, 0], ag.at[k, o], ag_ss.at[o], ag_rs.at[k, o], {"samp": flip(me, o)}
            )
        gf = gb.astype(F32)
        sm[k, me] = to_rows([row_sum(g * g), row_sum(gf * gf), row_sum(gf * d[0])])
        for o in peers:
            small[o] = send(
                sm.at[k, me], sm.at[k, me], sm_ss.at[o], sm_rs.at[k, o], {"samp": flip(me, o)}
            )
        for o in near:
            sent[o].wait_send()

        def image_of(o):
            return lax.dot_general(
                ag[k, o], a[o], (((1,), (1,)), ((), ())), preferred_element_type=F32
            )

        qa[...] = image_of(0)
        for o in near:
            gathered[o].wait_recv()
            qa[...] += image_of(o)

        c1_send[...] = qa[:, half:].astype(BF16)
        c1 = send(c1_send, c1_recv.at[k], f_ss.at[0], f_rs.at[k, 0], other_core)
        for o in near:
            small[o].wait_recv()
        sums = sm[k, 0]
        for i in range(1, n_samp):
            sums = sums + sm[k, i]
        c1s_send[...] = sums
        c1s = send(c1s_send, c1s_recv.at[k], f_ss.at[1], f_rs.at[k, 1], other_core)
        c1.wait()
        x2_send[...] = (qa[:, :half] + c1_recv[k].astype(F32)).astype(BF16)
        x2 = send(x2_send, x2_recv.at[k], f_ss.at[2], f_rs.at[k, 2], other_x)
        c1s.wait()
        sums = sums + c1s_recv[k]
        x2s_send[...] = sums
        x2s = send(x2s_send, x2s_recv.at[k], f_ss.at[3], f_rs.at[k, 3], other_x)
        for o in near:
            gathered[o].wait_send()
            small[o].wait_send()
        x2s.wait()
        sums = sums + x2s_recv[k]
        norm_next, gbsq, gd = to_columns(sums, 3)
        beta = jnp.where(k == 0, 0.0, norm_next / norm)
        dsq = gbsq + 2.0 * beta * gd + beta * beta * dsq
        x2.wait()
        mine = x2_send[...].astype(F32) + x2_recv[k].astype(F32) + beta * q[...]
        q[...] = mine
        c3 = send(q, c3_recv.at[k], f_ss.at[4], f_rs.at[k, 4], other_core)
        sq_mine = row_sum(mine * mine)
        c3.wait()
        theirs = c3_recv[k]
        cu[k, me] = to_rows([sq_mine + row_sum(theirs * theirs)])
        curved = {}
        for o in peers:
            curved[o] = send(
                cu.at[k, me], cu.at[k, me], cu_ss.at[o], cu_rs.at[k, o], {"samp": flip(me, o)}
            )
        for o in near:
            curved[o].wait()
        sums = cu[k, 0]
        for i in range(1, n_samp):
            sums = sums + cu[k, i]
        (image_sq,) = to_columns(sums, 1)
        alpha = norm_next / (image_sq + pen * dsq)
        r[0] = r[0] - alpha * q[...]
        r[1] = r[1] - alpha * c3_recv[k]
        return norm_next, dsq, alpha, beta

    one = jnp.ones_like(pen)
    zero = jnp.zeros_like(pen)
    _, _, alpha, beta = lax.fori_loop(0, ITERS, step, (one, zero, zero, zero))
    for h in range(2):
        r_out[:, pl.ds(pl.multiple_of(flip(core, h) * half, half), half)] = r[h]
    for o in range(n_samp):
        new = ag[ITERS - 1, o].astype(F32) + beta * d[o]
        columns = pl.ds(pl.multiple_of(flip(me, o) * chunk, chunk), chunk)
        x_out[:, columns] = x[o] + alpha * new


def fused(n_samp, states, targets, penalty):
    rows, columns = states.shape
    channels = targets.shape[1]
    chunk, half = columns // n_samp, rows // 2
    n, c = n_samp, channels
    dma = pltpu.SemaphoreType.DMA
    vmem = pltpu.VMEM
    x_t, r_t = pl.pallas_call(
        functools.partial(kernel, n_samp),
        out_shape=(
            jax.ShapeDtypeStruct((channels, columns), F32),
            jax.ShapeDtypeStruct((channels, rows), F32),
        ),
        in_specs=[
            pl.BlockSpec(memory_space=pl.ANY),
            pl.BlockSpec(memory_space=vmem),
            pl.BlockSpec(memory_space=vmem),
        ],
        out_specs=(pl.BlockSpec(memory_space=vmem), pl.BlockSpec(memory_space=vmem)),
        scratch_shapes=[
            vmem((n, rows, chunk), BF16),
            vmem((c, rows), BF16),
            vmem((2, c, half), F32),
            vmem((c, chunk), F32),
            vmem((n, c, chunk), BF16),
            vmem((ITERS, n, c, chunk), BF16),
            vmem((ITERS, n, c, chunk), BF16),
            vmem((n, c, chunk), F32),
            vmem((n, c, chunk), F32),
            vmem((c, rows), F32),
            vmem((c, half), F32),
            vmem((ITERS, n, 8, c), F32),
            vmem((ITERS, n, 8, c), F32),
            vmem((c, half), BF16),
            vmem((ITERS, c, half), BF16),
            vmem((8, c), F32),
            vmem((ITERS, 8, c), F32),
            vmem((c, half), BF16),
            vmem((ITERS, c, half), BF16),
            vmem((8, c), F32),
            vmem((ITERS, 8, c), F32),
            vmem((ITERS, c, half), F32),
            dma((n, 2)),
            dma((n,)), dma((ITERS, n)),
            dma((n,)), dma((ITERS, n)),
            dma((n,)), dma((ITERS, n)),
            dma((n,)), dma((ITERS, n)),
            dma((5,)), dma((ITERS, 5)),
        ],
        compiler_params=pltpu.CompilerParams(
            collective_id=0, has_side_effects=True, vmem_limit_bytes=52 * 1024 * 1024
        ),
        cost_estimate=pl.CostEstimate(
            flops=4 * ITERS * rows * columns * channels,
            bytes_accessed=2 * rows * columns + 8 * channels * (rows + columns),
            transcendentals=0,
        ),
    )(states, targets.T, penalty[:, None])
    return x_t.T, r_t.T


def plain(states, targets, penalty):
    feat_rows = states.shape[1]

    def weight_sum(value):
        return lax.psum(value, "feat")

    def gradient_of(residual, readout):
        residual_b = residual.astype(BF16)
        partial_value = lax.dot_general(
            states, residual_b, (((0,), (0,)), ((), ())), preferred_element_type=F32
        )
        return lax.psum(partial_value, "samp") - penalty * readout

    readout = jnp.zeros((feat_rows, targets.shape[1]), F32)
    residual = targets
    gradient = gradient_of(residual, readout)
    direction = gradient
    norm_now = weight_sum(jnp.sum(gradient * gradient, axis=0))
    for step in range(ITERS):
        image = lax.psum(
            jnp.dot(states, direction.astype(BF16), preferred_element_type=F32), "feat"
        )
        image_sq = jnp.sum(image * image, axis=0)
        direction_sq = jnp.sum(direction * direction, axis=0)
        curvature = lax.psum(image_sq, "samp") + penalty * weight_sum(direction_sq)
        step_size = norm_now / curvature
        readout = readout + step_size * direction
        residual = residual - step_size * image
        if step + 1 < ITERS:
            gradient = gradient_of(residual, readout)
            norm_next = weight_sum(jnp.sum(gradient * gradient, axis=0))
            direction = gradient + norm_next / norm_now * direction
            norm_now = norm_next
    return (readout, residual)


def solution(mesh):
    n_samp, n_feat = mesh.shape["samp"], mesh.shape["feat"]

    def shards(states, targets, penalty):
        rows, columns = states.shape
        fits = (
            n_samp & (n_samp - 1) == 0
            and n_feat == 4
            and columns % (128 * n_samp) == 0
            and rows % 256 == 0
            and targets.shape[1] == 128
        )
        if fits:
            return fused(n_samp, states, targets, penalty)
        return plain(states, targets, penalty)

    in_specs = (P("samp", "feat"), P("samp", None), P())
    out_specs = (P("feat", None), P("samp", None))
    return jax.shard_map(shards, mesh=mesh, in_specs=in_specs, out_specs=out_specs, check_vma=False)
```

time: 559 us -> 204 us (0.36)
  waiting for transfers between devices: 378 us -> 0 us
  Pallas kernels: 0 us -> 198 us
  blocking collectives: 95.1 us -> 0 us
  matrix products: 46.2 us -> 0 us
  other arithmetic: 21.3 us -> 0 us
  between operations: 14.2 us -> 0.65 us
    psum x6 -> x0, waiting for transfers between devices: 377 us -> none  [the longest x3 300 us: gradient_of(): summed = lax.psum(partial_value, 'samp')]
    pallas_call x0 -> x1, Pallas kernels: none -> 198 us  [fused(): pl.pallas_call(functools.partial(kernel, n_samp), out_shape=(jax.ShapeDty...]
    psum x8 -> x0, blocking collectives: 95.1 us -> none  [the longest x3 64.1 us: shards(): curvature = lax.psum(image_sq, 'samp') + penalty * weight_sum(direction_sq)]
    dot_general x6 -> x0, matrix products: 46.2 us -> none  [the longest x3 23.5 us: gradient_of(): lax.dot_general(states, residual_b, (((0,), (0,)), ((), ())), preferred_e...]
    reduce_sum x8 -> x0, other arithmetic: 14.6 us -> none  [the longest x2 5.4 us: shards(): direction_sq = jnp.sum(direction * direction, axis=0)]
  transfers between devices with their start and end apart: 6 -> 0, of which waited for: 6 -> 0; matrix products, arithmetic and copies ran while one was open for 1% -> 0% of each run, Pallas kernels for 0% -> 0%
where the time goes in v1:
time: 204 us
  Pallas kernels  198 us (97%)
  local copies, waits for them, and re-layouts  5.87 us (3%)
    pallas_call x1, Pallas kernels, fused(): pl.pallas_call(functools.partial(kernel, n_samp), out_shape=(jax.ShapeDty...  198 us
    unnamed x3, local copies, waits for them, and re-layouts  5.11 us

profile of v1, /device:TPU:0, one launch (start us, length us, event | category | flops | bytes accessed | tf_op | source)
XLA Modules:
  0.0 204.2 jit_solution(3259651026643446363)
XLA Ops:
  0.6 0.8 copy.6.pen_ref
  1.4 1.2 copy.5
  2.6 197.7 %shard_map.50 = (f32[128,4096]{1,0:T(8,128)}, f32[128,1024]{1,0:T(8,128)S(1)}) custom-call(bf16[1024,4096]{1,0:T(8,128)(2,1)} %a_hbm.1, f32[128,1024]{1,0:T(8,128)S(1)} %bitcast.5, f32[128,1]{1,0:T(8,128)S(1)} %copy.6.pen_ref), custom_call_target="tpu_custom_call" | custom-call | flops 6442450944 | bytes 13631488 | tf_op jit(solution)/shard_map/pallas_call | solution.py:218
  200.3 2.9 %copy.7 = f32[4096,128]{1,0:T(8,128)} copy(f32[4096,128]{0,1:T(8,128)} %bitcast.6) | data formatting | bytes 4194304
  203.2 1.0 copy.8

commit v2 on v1

--- a/solution.py
+++ b/solution.py
@@ -50,6 +50,9 @@
     core = feat % 2
     peers = sorted(range(1, n_samp), key=lambda o: (-(o // 4), o))
     near = list(range(1, n_samp))
+    far = [o for o in peers if o % 2 == 0]
+    line = [o for o in near if o % 2 == 0]
+    beside = {"samp": flip(me, 1)}
     other_core = {"feat": flip(feat, 1)}
     other_x = {"feat": flip(feat, 2)}
 
@@ -60,7 +63,7 @@
             a_hbm.at[rows, columns], a.at[o, pl.ds(h * half, half)], a_sem.at[o, h]
         )
 
-    for o in peers + [0]:
+    for o in [o + 1 for o in far + [0]] + far + [0]:
         for h in range(2):
             load(o, h).start()
 
@@ -106,12 +109,18 @@
 
             return jnp.dot(vb[...], a[o], preferred_element_type=F32)
 
-        sent = {}
-        for o in peers:
-            rs_send[o] = project(o).astype(BF16)
-            sent[o] = send(
-                rs_send.at[o], rs_recv.at[k, o], rs_ss.at[o], rs_rs.at[k, o], {"samp": flip(me, o)}
-            )
+        sent, gathered, small = {}, {}, {}
+
+        def scatter(o, value, target):
+            rs_send[o] = value.astype(BF16)
+            sent[o] = send(rs_send.at[o], rs_recv.at[k, o], rs_ss.at[o], rs_rs.at[k, o], target)
+
+        for o in far + [0]:
+            scatter(o + 1, project(o + 1), beside)
+        for o in far:
+            value = project(o)
+            sent[o + 1].wait_recv()
+            scatter(o, value + rs_recv[k, o + 1].astype(F32), {"samp": flip(me, o)})
         acc[...] = project(0)
 
         @pl.when(k > 0)
@@ -119,17 +128,19 @@
             for o in range(n_samp):
                 advance(o, k - 1, alpha, beta)
 
-        for o in near:
+        for o in [1] + line:
             sent[o].wait_recv()
             acc[...] += rs_recv[k, o].astype(F32)
         g = acc[...] - pen * x[0]
         gb = g.astype(BF16)
         ag[k, 0] = gb
-        gathered, small = {}, {}
-        for o in peers:
-            gathered[o] = send(
-                ag.at[k, 0], ag.at[k, o], ag_ss.at[o], ag_rs.at[k, o], {"samp": flip(me, o)}
-            )
+
+        def gather(src, o, target):
+            gathered[o] = send(ag.at[k, src], ag.at[k, o], ag_ss.at[o], ag_rs.at[k, o], target)
+
+        for o in far:
+            gather(0, o, {"samp": flip(me, o)})
+        gather(0, 1, beside)
         gf = gb.astype(F32)
         sm[k, me] = to_rows([row_sum(g * g), row_sum(gf * gf), row_sum(gf * d[0])])
         for o in peers:
@@ -145,8 +156,10 @@
             )
 
         qa[...] = image_of(0)
-        for o in near:
+        for o in line + [1] + [o + 1 for o in line]:
             gathered[o].wait_recv()
+            if o % 2 == 0:
+                gather(o, o + 1, beside)
             qa[...] += image_of(o)
 
         c1_send[...] = qa[:, half:].astype(BF16)

time: 204 us -> 158 us (0.77)
  Pallas kernels: 198 us -> 151 us
    pallas_call x1, Pallas kernels: 198 us -> 151 us  [fused(): pl.pallas_call(functools.partial(kernel, n_samp), out_shape=(jax.ShapeDty...]
where the time goes in v2:
time: 158 us
  Pallas kernels  151 us (96%)
  local copies, waits for them, and re-layouts  5.87 us (4%)
    pallas_call x1, Pallas kernels, fused(): pl.pallas_call(functools.partial(kernel, n_samp), out_shape=(jax.ShapeDty...  151 us
    unnamed x3, local copies, waits for them, and re-layouts  5.11 us

profile of v2, /device:TPU:0, one launch (start us, length us, event | category | flops | bytes accessed | tf_op | source)
XLA Modules:
  0.0 157.7 jit_solution(17280714034803839827)
XLA Ops:
  0.6 0.8 copy.6.pen_ref
  1.4 1.2 copy.5
  2.6 151.2 %shard_map.50 = (f32[128,4096]{1,0:T(8,128)}, f32[128,1024]{1,0:T(8,128)S(1)}) custom-call(bf16[1024,4096]{1,0:T(8,128)(2,1)} %a_hbm.1, f32[128,1024]{1,0:T(8,128)S(1)} %bitcast.5, f32[128,1]{1,0:T(8,128)S(1)} %copy.6.pen_ref), custom_call_target="tpu_custom_call" | custom-call | flops 6442450944 | bytes 13631488 | tf_op jit(solution)/shard_map/pallas_call | solution.py:231
  153.8 2.9 %copy.7 = f32[4096,128]{1,0:T(8,128)} copy(f32[4096,128]{0,1:T(8,128)} %bitcast.6) | data formatting | bytes 4194304
  156.7 1.0 copy.8

commit v3 on v2

--- a/solution.py
+++ b/solution.py
@@ -50,8 +50,7 @@
     core = feat % 2
     peers = sorted(range(1, n_samp), key=lambda o: (-(o // 4), o))
     near = list(range(1, n_samp))
-    far = [o for o in peers if o % 2 == 0]
-    line = [o for o in near if o % 2 == 0]
+    far = [6, 4, 2]
     beside = {"samp": flip(me, 1)}
     other_core = {"feat": flip(feat, 1)}
     other_x = {"feat": flip(feat, 2)}
@@ -120,7 +119,11 @@
         for o in far:
             value = project(o)
             sent[o + 1].wait_recv()
-            scatter(o, value + rs_recv[k, o + 1].astype(F32), {"samp": flip(me, o)})
+            value = value + rs_recv[k, o + 1].astype(F32)
+            if o == 4:
+                sent[6].wait_recv()
+                value = value + rs_recv[k, 6].astype(F32)
+            scatter(o, value, {"samp": flip(me, 4 if o == 4 else 2)})
         acc[...] = project(0)
 
         @pl.when(k > 0)
@@ -128,7 +131,7 @@
             for o in range(n_samp):
                 advance(o, k - 1, alpha, beta)
 
-        for o in [1] + line:
+        for o in (1, 2, 4):
             sent[o].wait_recv()
             acc[...] += rs_recv[k, o].astype(F32)
         g = acc[...] - pen * x[0]
@@ -138,7 +141,7 @@
         def gather(src, o, target):
             gathered[o] = send(ag.at[k, src], ag.at[k, o], ag_ss.at[o], ag_rs.at[k, o], target)
 
-        for o in far:
+        for o in (4, 2):
             gather(0, o, {"samp": flip(me, o)})
         gather(0, 1, beside)
         gf = gb.astype(F32)
@@ -156,8 +159,10 @@
             )
 
         qa[...] = image_of(0)
-        for o in line + [1] + [o + 1 for o in line]:
+        for o in (2, 4, 1, 3, 6, 5, 7):
             gathered[o].wait_recv()
+            if o == 4:
+                gather(4, 6, {"samp": flip(me, 2)})
             if o % 2 == 0:
                 gather(o, o + 1, beside)
             qa[...] += image_of(o)
@@ -324,7 +329,7 @@
     def shards(states, targets, penalty):
         rows, columns = states.shape
         fits = (
-            n_samp & (n_samp - 1) == 0
+            n_samp == 8
             and n_feat == 4
             and columns % (128 * n_samp) == 0
             and rows % 256 == 0

time: 158 us -> 161 us (1.019)
  Pallas kernels: 151 us -> 154 us
    pallas_call x1, Pallas kernels: 151 us -> 154 us  [fused(): pl.pallas_call(functools.partial(kernel, n_samp), out_shape=(jax.ShapeDty...]
where the time goes in v3:
time: 161 us
  Pallas kernels  154 us (96%)
  local copies, waits for them, and re-layouts  5.87 us (4%)
    pallas_call x1, Pallas kernels, fused(): pl.pallas_call(functools.partial(kernel, n_samp), out_shape=(jax.ShapeDty...  154 us
    unnamed x3, local copies, waits for them, and re-layouts  5.11 us

profile of v3, /device:TPU:0, one launch (start us, length us, event | category | flops | bytes accessed | tf_op | source)
XLA Modules:
  0.0 160.9 jit_solution(13401867171183506090)
XLA Ops:
  0.6 0.8 copy.6.pen_ref
  1.4 1.2 copy.5
  2.6 154.4 %shard_map.50 = (f32[128,4096]{1,0:T(8,128)}, f32[128,1024]{1,0:T(8,128)S(1)}) custom-call(bf16[1024,4096]{1,0:T(8,128)(2,1)} %a_hbm.1, f32[128,1024]{1,0:T(8,128)S(1)} %bitcast.5, f32[128,1]{1,0:T(8,128)S(1)} %copy.6.pen_ref), custom_call_target="tpu_custom_call" | custom-call | flops 6442450944 | bytes 13631488 | tf_op jit(solution)/shard_map/pallas_call | solution.py:236
  157.1 2.9 %copy.7 = f32[4096,128]{1,0:T(8,128)} copy(f32[4096,128]{0,1:T(8,128)} %bitcast.6) | data formatting | bytes 4194304
  160.0 1.0 copy.8

commit v4 on v2

--- a/solution.py
+++ b/solution.py
@@ -138,9 +138,9 @@
         def gather(src, o, target):
             gathered[o] = send(ag.at[k, src], ag.at[k, o], ag_ss.at[o], ag_rs.at[k, o], target)
 
-        for o in far:
+        gather(0, 1, beside)
+        for o in line:
             gather(0, o, {"samp": flip(me, o)})
-        gather(0, 1, beside)
         gf = gb.astype(F32)
         sm[k, me] = to_rows([row_sum(g * g), row_sum(gf * gf), row_sum(gf * d[0])])
         for o in peers:
@@ -156,10 +156,12 @@
             )
 
         qa[...] = image_of(0)
+        for o in line:
+            gathered[o].wait_recv()
+            gather(o, o + 1, beside)
         for o in line + [1] + [o + 1 for o in line]:
-            gathered[o].wait_recv()
-            if o % 2 == 0:
-                gather(o, o + 1, beside)
+            if o % 2 == 1:
+                gathered[o].wait_recv()
             qa[...] += image_of(o)
 
         c1_send[...] = qa[:, half:].astype(BF16)

time: 158 us -> 155 us (0.981)
  Pallas kernels: 151 us -> 148 us
    pallas_call x1, Pallas kernels: 151 us -> 148 us  [fused(): pl.pallas_call(functools.partial(kernel, n_samp), out_shape=(jax.ShapeDty...]
where the time goes in v4:
time: 155 us
  Pallas kernels  148 us (95%)
  local copies, waits for them, and re-layouts  5.87 us (4%)
    pallas_call x1, Pallas kernels, fused(): pl.pallas_call(functools.partial(kernel, n_samp), out_shape=(jax.ShapeDty...  148 us
    unnamed x3, local copies, waits for them, and re-layouts  5.11 us

profile of v4, /device:TPU:0, one launch (start us, length us, event | category | flops | bytes accessed | tf_op | source)
XLA Modules:
  0.0 154.7 jit_solution(10450102883300559007)
XLA Ops:
  0.6 0.8 copy.6.pen_ref
  1.4 1.2 copy.5
  2.6 148.2 %shard_map.50 = (f32[128,4096]{1,0:T(8,128)}, f32[128,1024]{1,0:T(8,128)S(1)}) custom-call(bf16[1024,4096]{1,0:T(8,128)(2,1)} %a_hbm.1, f32[128,1024]{1,0:T(8,128)S(1)} %bitcast.5, f32[128,1]{1,0:T(8,128)S(1)} %copy.6.pen_ref), custom_call_target="tpu_custom_call" | custom-call | flops 6442450944 | bytes 13631488 | tf_op jit(solution)/shard_map/pallas_call | solution.py:233
  150.8 2.9 %copy.7 = f32[4096,128]{1,0:T(8,128)} copy(f32[4096,128]{0,1:T(8,128)} %bitcast.6) | data formatting | bytes 4194304
  153.7 1.0 copy.8

commit v5 on v4

--- a/solution.py
+++ b/solution.py
@@ -53,6 +53,7 @@
     far = [o for o in peers if o % 2 == 0]
     line = [o for o in near if o % 2 == 0]
     beside = {"samp": flip(me, 1)}
+    along = {"samp": flip(me, 2)}
     other_core = {"feat": flip(feat, 1)}
     other_x = {"feat": flip(feat, 2)}
 
@@ -115,12 +116,17 @@
             rs_send[o] = value.astype(BF16)
             sent[o] = send(rs_send.at[o], rs_recv.at[k, o], rs_ss.at[o], rs_rs.at[k, o], target)
 
-        for o in far + [0]:
+        for o in (4, 6):
             scatter(o + 1, project(o + 1), beside)
-        for o in far:
+        scatter(3, project(3), along)
+        for o in (4, 6):
             value = project(o)
             sent[o + 1].wait_recv()
             scatter(o, value + rs_recv[k, o + 1].astype(F32), {"samp": flip(me, o)})
+        value = project(1)
+        sent[3].wait_recv()
+        scatter(1, value + rs_recv[k, 3].astype(F32), beside)
+        scatter(2, project(2), along)
         acc[...] = project(0)
 
         @pl.when(k > 0)
@@ -156,11 +162,14 @@
             )
 
         qa[...] = image_of(0)
+        gathered[1].wait_recv()
+        gather(1, 3, along)
         for o in line:
             gathered[o].wait_recv()
-            gather(o, o + 1, beside)
+            if o > 2:
+                gather(o, o + 1, beside)
         for o in line + [1] + [o + 1 for o in line]:
-            if o % 2 == 1:
+            if o in (3, 5, 7):
                 gathered[o].wait_recv()
             qa[...] += image_of(o)
 
@@ -326,7 +335,7 @@
     def shards(states, targets, penalty):
         rows, columns = states.shape
         fits = (
-            n_samp & (n_samp - 1) == 0
+            n_samp == 8
             and n_feat == 4
             and columns % (128 * n_samp) == 0
             and rows % 256 == 0

time: 155 us -> 154 us (level)
  no operation moved by 1% of the time
where the time goes in v5:
time: 154 us; the launch traced here: 153 us
  Pallas kernels  147 us (95%)
  local copies, waits for them, and re-layouts  5.87 us (4%)
    pallas_call x1, Pallas kernels, fused(): pl.pallas_call(functools.partial(kernel, n_samp), out_shape=(jax.ShapeDty...  147 us
    unnamed x3, local copies, waits for them, and re-layouts  5.11 us

profile of v5, /device:TPU:0, one launch (start us, length us, event | category | flops | bytes accessed | tf_op | source)
XLA Modules:
  0.0 153.4 jit_solution(9216433379478779505)
XLA Ops:
  0.6 0.8 copy.6.pen_ref
  1.4 1.2 copy.5
  2.6 146.9 %shard_map.50 = (f32[128,4096]{1,0:T(8,128)}, f32[128,1024]{1,0:T(8,128)S(1)}) custom-call(bf16[1024,4096]{1,0:T(8,128)(2,1)} %a_hbm.1, f32[128,1024]{1,0:T(8,128)S(1)} %bitcast.5, f32[128,1]{1,0:T(8,128)S(1)} %copy.6.pen_ref), custom_call_target="tpu_custom_call" | custom-call | flops 6442450944 | bytes 13631488 | tf_op jit(solution)/shard_map/pallas_call | solution.py:242
  149.5 2.9 %copy.7 = f32[4096,128]{1,0:T(8,128)} copy(f32[4096,128]{0,1:T(8,128)} %bitcast.6) | data formatting | bytes 4194304
  152.4 1.0 copy.8
